TPU v7x, 256 devices: a whole 4x4x8 slice. The times are simulated.
256 devices in a mesh: section: 8 (over z_lo, core), expert: 16 (over y, x), dp: 2 (over z_hi).
Axes of the slice: x: 4, y: 4, z: 8 (z_hi: 2, z_lo: 4; z = z_hi * 4 + z_lo), core: 2. Of those that a mesh axis runs over, the one named last changes fastest.
Arguments:
- fwd_input: bfloat16 [8, 4096, 3584], P('section', ('expert', 'dp')), may hold values from -6 to 6
- fwd_routes: int32 [8, 4096, 1], P('section', ('expert', 'dp')), may hold values from 0 to 7; in each aligned block of 128 rows (0 to 127, 128 to 255, ..., all dimensions but the last counted through in order) at most 24 rows name the same one
- fwd_gates: int32 [8, 4096, 1], P('section', ('expert', 'dp')), may hold values from 1 to 65535
- bwd_input: bfloat16 [8, 4096, 3584], P('section', ('expert', 'dp')), may hold values from -6 to 6
- bwd_cotangent: bfloat16 [8, 4096, 3584], P('section', ('expert', 'dp')), may hold values from -6 to 6
- bwd_routes: int32 [8, 4096, 1], P('section', ('expert', 'dp')), may hold values from 0 to 7; in each aligned block of 128 rows (0 to 127, 128 to 255, ..., all dimensions but the last counted through in order) at most 24 rows name the same one
- bwd_gates: int32 [8, 4096, 1], P('section', ('expert', 'dp')), may hold values from 1 to 65535
- norm_gain: float32 [8, 3584], P('section'), may hold values from 0.5 to 1.5
- w_gate: bfloat16 [8, 16, 3584, 512], P('section', 'expert', 'dp'), may hold values from -0.09375 to 0.09375
- w_up: bfloat16 [8, 16, 3584, 512], P('section', 'expert', 'dp'), may hold values from -0.09375 to 0.09375
- w_down: bfloat16 [8, 16, 512, 3584], P('section', 'expert', 'dp'), may hold values from -0.1875 to 0.1875
Outputs:
- fwd_next: bfloat16 [8, 4096, 3584], P('section', ('expert', 'dp'))
- bwd_next: bfloat16 [8, 4096, 3584], P('section', ('expert', 'dp'))
- gain_grad: float32 [8, 3584], P('section')
Inputs may be any that keep to these rules, and one draw needn't show every extreme that they name: `fwd_routes`: each token names 1 different experts; among the 128 rows of one device no expert is named more than 24 times, a bound that some block reaches. `bwd_routes`: each token names 1 different experts; among the 128 rows of one device no expert is named more than 24 times, a bound that some block reaches.
All inputs are finite; a program needn't handle non-finite values.
Results may differ from a plain program's by a relative error of at most 0.0073.
Values may be sent and summed in bfloat16 or wider, within the bound.
A program may use at most 128 MiB of HBM per device.

v0:
```python
import jax
import jax.numpy as jnp
from jax import lax
from jax.sharding import PartitionSpec as P

eps = 1e-06
fixed_scale = 65536.0


def shifted(value, axis, steps):
    count = lax.axis_size(axis)
    pairs = [(source, (source + steps) % count) for source in range(count)]
    return lax.ppermute(value, axis, pairs)


def slot_positions(route_block, experts, capacity):
    flat_ids = route_block.reshape(-1)
    onehot = (flat_ids[:, None] == jnp.arange(experts, dtype=jnp.int32)[None, :]).astype(jnp.int32)
    earlier = jnp.cumsum(onehot, axis=0) - onehot
    order_rank = jnp.sum(earlier * onehot, axis=1)
    return flat_ids * capacity + order_rank


def place_rows(row_data, slot_index, experts, capacity):
    width = row_data.shape[-1]
    filled = jnp.zeros((experts * capacity, width), row_data.dtype).at[slot_index].set(row_data)
    filled = filled.reshape(experts, capacity, width)
    return jnp.repeat(filled, 2, axis=0)


def normalize(inputs, gain_row):
    values = inputs.astype(jnp.float32)
    inverse = lax.rsqrt(jnp.mean(values * values, axis=-1, keepdims=True) + eps)
    return (values, inverse, (values * inverse * gain_row).astype(jnp.bfloat16))


def expert_forward(block, gate_mat, up_mat, down_mat):
    shape_in = block.shape
    flat_rows = block.reshape(-1, shape_in[-1])
    gate_act = jnp.dot(flat_rows, gate_mat, preferred_element_type=jnp.float32)
    up_act = jnp.dot(flat_rows, up_mat, preferred_element_type=jnp.float32)
    hidden_act = (jax.nn.silu(gate_act) * up_act).astype(jnp.bfloat16)
    result = jnp.dot(hidden_act, down_mat, preferred_element_type=jnp.float32).astype(jnp.bfloat16)
    return result.reshape(shape_in)


def expert_backward(block_in, block_cot, gate_mat, up_mat, down_mat):
    shape_in = block_in.shape
    flat_in = block_in.reshape(-1, shape_in[-1])
    flat_cot = block_cot.reshape(-1, shape_in[-1])
    last_dims = (((1,), (1,)), ((), ()))
    gate_act = jnp.dot(flat_in, gate_mat, preferred_element_type=jnp.float32)
    up_act = jnp.dot(flat_in, up_mat, preferred_element_type=jnp.float32)
    sigma = jax.nn.sigmoid(gate_act)
    silu_val = gate_act * sigma
    act_grad = lax.dot_general(flat_cot, down_mat, last_dims, preferred_element_type=jnp.float32)
    up_pre = (act_grad * silu_val).astype(jnp.bfloat16)
    gate_pre = (act_grad * up_act * sigma * (1.0 + gate_act * (1.0 - sigma))).astype(jnp.bfloat16)
    route_grad = lax.dot_general(gate_pre, gate_mat, last_dims, preferred_element_type=jnp.float32)
    route_grad = route_grad + lax.dot_general(
        up_pre, up_mat, last_dims, preferred_element_type=jnp.float32
    )
    return route_grad.astype(jnp.bfloat16).reshape(shape_in)


def combine_halves(partial_value, half_cap, experts):
    width = partial_value.shape[-1]
    back = lax.all_to_all(partial_value, "expert", split_axis=0, concat_axis=0, tiled=True)
    both = back.reshape(experts, 2, 2 * half_cap, width).astype(jnp.float32)
    return (both[:, 0] + both[:, 1]).astype(jnp.bfloat16).reshape(experts * 2 * half_cap, width)


def on_device(
    fwd_input,
    fwd_routes,
    fwd_gates,
    bwd_input,
    bwd_cotangent,
    bwd_routes,
    bwd_gates,
    norm_gain,
    w_gate,
    w_up,
    w_down,
):
    experts = lax.axis_size("expert") // 2
    tok_count = fwd_input.shape[1]
    top_count = fwd_routes.shape[2]
    capacity = 2 * (3 * tok_count * top_count // (4 * experts))
    half_cap = capacity // 2
    gain_row = norm_gain[0]
    gate_all, up_all, down_all = (
        lax.all_gather(w_gate, "dp", axis=2, tiled=True),
        lax.all_gather(w_up, "dp", axis=2, tiled=True),
        lax.all_gather(w_down, "dp", axis=2, tiled=True),
    )
    gate_mat = gate_all[0, 0]
    up_mat = up_all[0, 0]
    down_mat = down_all[0, 0]
    fwd_values, fwd_inverse, fwd_normed = normalize(fwd_input[0], gain_row)
    fwd_slots = slot_positions(fwd_routes[0], experts, capacity)
    fwd_buffer = place_rows(jnp.repeat(fwd_normed, top_count, axis=0), fwd_slots, experts, capacity)
    bwd_values, bwd_inverse, bwd_normed = normalize(bwd_input[0], gain_row)
    bwd_slots = slot_positions(bwd_routes[0], experts, capacity)
    bwd_weights = bwd_gates[0].astype(jnp.float32) / fixed_scale
    cotangent = bwd_cotangent[0].astype(jnp.float32)
    route_cot = (jnp.repeat(cotangent, top_count, axis=0) * bwd_weights).astype(jnp.bfloat16)
    bwd_in_buffer = place_rows(
        jnp.repeat(bwd_normed, top_count, axis=0), bwd_slots, experts, capacity
    )
    bwd_cot_buffer = place_rows(route_cot, bwd_slots, experts, capacity)
    recv_fwd = lax.all_to_all(fwd_buffer, "expert", split_axis=0, concat_axis=0, tiled=True)
    recv_in, recv_cot = (
        lax.all_to_all(bwd_in_buffer, "expert", split_axis=0, concat_axis=0, tiled=True),
        lax.all_to_all(bwd_cot_buffer, "expert", split_axis=0, concat_axis=0, tiled=True),
    )
    recv_fwd, recv_in, recv_cot = (recv_fwd, recv_in, recv_cot)
    fwd_part = expert_forward(recv_fwd, gate_mat, up_mat, down_mat)
    grad_part = expert_backward(recv_in, recv_cot, gate_mat, up_mat, down_mat)
    fwd_back = combine_halves(fwd_part, half_cap, experts)
    bwd_back = combine_halves(grad_part, half_cap, experts)
    width = fwd_values.shape[-1]
    fwd_picked = fwd_back[fwd_slots].reshape(tok_count, top_count, width)
    fwd_weights = fwd_gates[0].astype(jnp.float32) / fixed_scale
    mixed = jnp.sum(fwd_weights[:, :, None] * fwd_picked.astype(jnp.float32), axis=1)
    layer_out = (fwd_values + mixed).astype(jnp.bfloat16)
    fwd_next = shifted(layer_out[None], "section", 1)
    bwd_picked = bwd_back[bwd_slots].reshape(tok_count, top_count, width)
    normed_grad = jnp.sum(bwd_picked.astype(jnp.float32), axis=1)
    gain_local = jnp.sum(normed_grad * bwd_values * bwd_inverse, axis=0)
    scaled = normed_grad * gain_row
    inner_mean = jnp.mean(scaled * bwd_values, axis=-1, keepdims=True)
    input_grad = bwd_inverse * (scaled - bwd_values * bwd_inverse * bwd_inverse * inner_mean)
    total_grad = (cotangent + input_grad).astype(jnp.bfloat16)
    bwd_next = shifted(total_grad[None], "section", -1)
    gain_grad = lax.psum(gain_local, ("expert", "dp"))
    return (fwd_next, bwd_next, gain_grad[None])


def solution(mesh):
    placed = (
        P("section", ("expert", "dp"), None),
        P("section", ("expert", "dp"), None),
        P("section", ("expert", "dp"), None),
        P("section", ("expert", "dp"), None),
        P("section", ("expert", "dp"), None),
        P("section", ("expert", "dp"), None),
        P("section", ("expert", "dp"), None),
        P("section", None),
        P("section", "expert", "dp", None),
        P("section", "expert", "dp", None),
        P("section", "expert", "dp", None),
    )
    return jax.shard_map(
        on_device,
        mesh=mesh,
        in_specs=placed,
        out_specs=(
            P("section", ("expert", "dp"), None),
            P("section", ("expert", "dp"), None),
            P("section", None),
        ),
        check_vma=False,
    )
```

profile of v0, /device:TPU:2, one launch (start us, length us, event | category | flops | bytes accessed | tf_op | source)
XLA Modules:
  0.0 646.0 jit_solution(6045701617904490949)
XLA Ops:
  9.5 2.4 scatter_custom_fusion
  13.6 7.6 %all-to-all-start = ((bf16[16,24,3584]{2,1,0:T(8,128)(2,1)}), bf16[16,24,3584]{2,1,0:T(8,128)(2,1)}, u32[]{:S(2)}, u32[]{:S(2)}) async-start(bf16[16,24,3584]{2,1,0:T(8,128)(2,1)} %bitcast.7), calls=%async_computation | async-start | bytes 5505024 | tf_op jit(solution)/shard_map/all_to_all | solution.py:112
  21.7 2.4 scatter_custom_fusion.1
  24.1 34.0 %all-to-all-done = bf16[16,24,3584]{2,1,0:T(8,128)(2,1)} async-done(((bf16[16,24,3584]{2,1,0:T(8,128)(2,1)}), bf16[16,24,3584]{2,1,0:T(8,128)(2,1)}, u32[]{:S(2)}, u32[]{:S(2)}) %all-to-all-start) | async-done | bytes 2752544 | tf_op jit(solution)/shard_map/all_to_all | solution.py:112
  59.8 9.3 %all-to-all-start.2 = ((bf16[16,24,3584]{2,1,0:T(8,128)(2,1)}), bf16[16,24,3584]{2,1,0:T(8,128)(2,1)}, u32[]{:S(2)}, u32[]{:S(2)}) async-start(bf16[16,24,3584]{2,1,0:T(8,128)(2,1)} %bitcast.154), calls=%async_computation.2 | async-start | bytes 5505024 | tf_op jit(solution)/shard_map/all_to_all | solution.py:115
  70.2 2.4 scatter_custom_fusion.2
  72.6 30.5 %all-to-all-done.2 = bf16[16,24,3584]{2,1,0:T(8,128)(2,1)} async-done(((bf16[16,24,3584]{2,1,0:T(8,128)(2,1)}), bf16[16,24,3584]{2,1,0:T(8,128)(2,1)}, u32[]{:S(2)}, u32[]{:S(2)}) %all-to-all-start.2) | async-done | bytes 2752544 | tf_op jit(solution)/shard_map/all_to_all | solution.py:115
  104.9 9.5 %all-to-all-start.3 = ((bf16[16,24,3584]{2,1,0:T(8,128)(2,1)}), bf16[16,24,3584]{2,1,0:T(8,128)(2,1)}, u32[]{:S(2)}, u32[]{:S(2)}) async-start(bf16[16,24,3584]{2,1,0:T(8,128)(2,1)} %bitcast.155), calls=%async_computation.3 | async-start | bytes 5505024 | tf_op jit(solution)/shard_map/all_to_all | solution.py:114
  114.5 4.4 fusion.13
  118.9 92.3 %all-gather.8.cloned.1.call-done = bf16[1,1,512,3584]{3,2,1,0:T(8,128)(2,1)} async-done(((bf16[1,1,256,3584]{3,2,1,0:T(8,128)(2,1)}), bf16[1,1,512,3584]{3,2,1,0:T(8,128)(2,1)}) %all-gather.8.cloned.1.call-update) | async-done | bytes 3670032 | tf_op jit(solution)/shard_map/all_gather | solution.py:95
  211.3 98.2 %all-gather.6.cloned.1.call-done = bf16[1,1,3584,512]{3,2,1,0:T(8,128)(2,1)} async-done(((bf16[1,1,1792,512]{3,2,1,0:T(8,128)(2,1)}), bf16[1,1,3584,512]{3,2,1,0:T(8,128)(2,1)}) %all-gather.6.cloned.1.call-update) | async-done | bytes 3670032 | tf_op jit(solution)/shard_map/all_gather | solution.py:94
  309.5 8.6 %convolution_convert_fusion = bf16[384,3584]{1,0:T(8,128)(2,1)} fusion(bf16[1,1,512,3584]{3,2,1,0:T(8,128)(2,1)} %all-gather.8.cloned.1.call-done, bf16[384,3584]{1,0:T(8,128)(2,1)} %bitcast.8, bf16[1,1,3584,512]{3,2,1,0:T(8,128)(2,1)} %all-gather.6.cloned.1.call-done, f32[384,512]{1,0:T(8,128)S(1)} %fusion.13), kind=kOutput, calls=%fused_computation.7 | convolution fusion | flops 2821128192 | bytes 13631488 | tf_op jit(solution)/shard_map/dot_general | solution.py:43
  318.1 7.3 %all-to-all-start.1 = ((bf16[16,24,3584]{2,1,0:T(8,128)(2,1)}), bf16[16,24,3584]{2,1,0:T(8,128)(2,1)}, u32[]{:S(2)}, u32[]{:S(2)}) async-start(bf16[16,24,3584]{2,1,0:T(8,128)(2,1)} %bitcast.159), calls=%async_computation.1 | async-start | bytes 5505024 | tf_op jit(solution)/shard_map/all_to_all | solution.py:68
  325.3 4.6 fusion.1
  330.0 3.4 fusion.11
  333.3 9.5 %fusion.9 = f32[384,3584]{1,0:T(8,128)} fusion(bf16[1,1,3584,512]{3,2,1,0:T(8,128)(2,1)} %all-gather.4.cloned.1.call-done, f32[384,512]{1,0:T(8,128)S(1)} %fusion.1, bf16[384,3584]{1,0:T(8,128)(2,1)} %bitcast.29, bf16[1,1,3584,512]{3,2,1,0:T(8,128)(2,1)} %all-gather.6.cloned.1.call-done, f32[384,512]{1,0:T(8,128)S(1)} %fusion.11), kind=kOutput, calls=%fused_computation.16 | convolution fusion | flops 2820538368 | bytes 17170432 | tf_op jit(solution)/shard_map/dot_general | solution.py:59
  342.9 6.8 %fusion = bf16[384,3584]{1,0:T(8,128)(2,1)} fusion(f32[384,3584]{1,0:T(8,128)} %fusion.9, bf16[1,1,3584,512]{3,2,1,0:T(8,128)(2,1)} %all-gather.6.cloned.1.call-done, f32[384,512]{1,0:T(8,128)S(1)} %fusion.1, f32[384,512]{1,0:T(8,128)S(1)} %fusion.11), kind=kOutput, calls=%fused_computation.6 | convolution fusion | flops 1413218304 | bytes 13500416 | tf_op jit(solution)/shard_map/dot_general | solution.py:60
  349.7 12.3 %all-to-all-done.1 = bf16[16,24,3584]{2,1,0:T(8,128)(2,1)} async-done(((bf16[16,24,3584]{2,1,0:T(8,128)(2,1)}), bf16[16,24,3584]{2,1,0:T(8,128)(2,1)}, u32[]{:S(2)}, u32[]{:S(2)}) %all-to-all-start.1) | async-done | bytes 2752544 | tf_op jit(solution)/shard_map/all_to_all | solution.py:68
  362.1 9.4 %all-to-all-start.4 = ((bf16[16,24,3584]{2,1,0:T(8,128)(2,1)}), bf16[16,24,3584]{2,1,0:T(8,128)(2,1)}, u32[]{:S(2)}, u32[]{:S(2)}) async-start(bf16[16,24,3584]{2,1,0:T(8,128)(2,1)} %bitcast.153), calls=%async_computation.4 | async-start | bytes 5505024 | tf_op jit(solution)/shard_map/all_to_all | solution.py:68
  371.5 2.4 convert.7
  376.3 2.4 fusion.27
  378.7 26.6 %all-to-all-done.4 = bf16[16,24,3584]{2,1,0:T(8,128)(2,1)} async-done(((bf16[16,24,3584]{2,1,0:T(8,128)(2,1)}), bf16[16,24,3584]{2,1,0:T(8,128)(2,1)}, u32[]{:S(2)}, u32[]{:S(2)}) %all-to-all-start.4) | async-done | bytes 2752544 | tf_op jit(solution)/shard_map/all_to_all | solution.py:68
  405.3 2.4 convert.8
  411.9 224.5 %psum.7 = f32[1,3584]{1,0:T(1,128)} all-reduce(f32[1,3584]{1,0:T(1,128)S(1)} %broadcast_in_dim.11), channel_id=1, replica_groups=mesh['section'=8,'expert'=16,'dp'=2] {'expert','dp'}, use_global_device_ids=true, to_apply=%region_11.12 | all-reduce | flops 3584 | bytes 28672 | tf_op jit(solution)/shard_map/psum | solution.py:136
  (60 shorter events, 18.5 us)
Async XLA Ops:
  7.2 1.5 copy-start.4
  7.2 1.6 copy-start.1
  7.2 2.2 copy-start.3
  7.2 107.2 %all-gather.4.cloned.1.call-start = ((), (), s32[]{:S(2)}) async-start(), calls=%async_computation.5 | async-start | bytes 5505024 | tf_op jit(solution)/shard_map/all_gather | solution.py:93
  7.9 203.3 %all-gather.8.cloned.1.call-start = ((), (), s32[]{:S(2)}) async-start(), calls=%async_computation.7 | async-start | bytes 5505024 | tf_op jit(solution)/shard_map/all_gather | solution.py:95
  13.6 7.6 %copy-start.5 = (s32[1,128,1]{1,2,0:T(1,128)S(1)}, s32[1,128,1]{1,2,0:T(1,128)}, u32[]{:S(2)}) copy-start(s32[1,128,1]{1,2,0:T(1,128)} %param.16) | copy-start | bytes 1540
  13.6 8.1 %copy-start.7 = (s32[1,128,1]{1,2,0:T(1,128)S(1)}, s32[1,128,1]{1,2,0:T(1,128)}, u32[]{:S(2)}) copy-start(s32[1,128,1]{1,2,0:T(1,128)} %param.17) | copy-start | bytes 1540
  13.6 8.1 %copy-start.2 = (bf16[1,128,3584]{2,1,0:T(8,128)(2,1)S(1)}, bf16[1,128,3584]{2,1,0:T(8,128)(2,1)}, u32[]{:S(2)}) copy-start(bf16[1,128,3584]{2,1,0:T(8,128)(2,1)} %param.15) | copy-start | bytes 2752516
  13.6 44.5 %all-to-all-start = ((bf16[16,24,3584]{2,1,0:T(8,128)(2,1)}), bf16[16,24,3584]{2,1,0:T(8,128)(2,1)}, u32[]{:S(2)}, u32[]{:S(2)}) async-start(bf16[16,24,3584]{2,1,0:T(8,128)(2,1)} %bitcast.7), calls=%async_computation | async-start | bytes 5505024 | tf_op jit(solution)/shard_map/all_to_all | solution.py:112
  59.8 10.1 %copy-start = (bf16[1,128,3584]{2,1,0:T(8,128)(2,1)S(1)}, bf16[1,128,3584]{2,1,0:T(8,128)(2,1)}, u32[]{:S(2)}) copy-start(bf16[1,128,3584]{2,1,0:T(8,128)(2,1)} %param.14) | copy-start | bytes 2752516
  59.8 43.3 %all-to-all-start.2 = ((bf16[16,24,3584]{2,1,0:T(8,128)(2,1)}), bf16[16,24,3584]{2,1,0:T(8,128)(2,1)}, u32[]{:S(2)}, u32[]{:S(2)}) async-start(bf16[16,24,3584]{2,1,0:T(8,128)(2,1)} %bitcast.154), calls=%async_computation.2 | async-start | bytes 5505024 | tf_op jit(solution)/shard_map/all_to_all | solution.py:115
  69.2 240.3 %all-gather.6.cloned.1.call-start = ((), (), s32[]{:S(2)}) async-start(), calls=%async_computation.6 | async-start | bytes 5505024 | tf_op jit(solution)/shard_map/all_gather | solution.py:94
  104.9 213.1 %all-to-all-start.3 = ((bf16[16,24,3584]{2,1,0:T(8,128)(2,1)}), bf16[16,24,3584]{2,1,0:T(8,128)(2,1)}, u32[]{:S(2)}, u32[]{:S(2)}) async-start(bf16[16,24,3584]{2,1,0:T(8,128)(2,1)} %bitcast.155), calls=%async_computation.3 | async-start | bytes 5505024 | tf_op jit(solution)/shard_map/all_to_all | solution.py:114
  318.1 44.0 %all-to-all-start.1 = ((bf16[16,24,3584]{2,1,0:T(8,128)(2,1)}), bf16[16,24,3584]{2,1,0:T(8,128)(2,1)}, u32[]{:S(2)}, u32[]{:S(2)}) async-start(bf16[16,24,3584]{2,1,0:T(8,128)(2,1)} %bitcast.159), calls=%async_computation.1 | async-start | bytes 5505024 | tf_op jit(solution)/shard_map/all_to_all | solution.py:68
  325.3 4.6 copy-start.6
  362.1 9.4 %copy-start.8 = (s32[1,128,1]{1,2,0:T(1,128)S(1)}, s32[1,128,1]{1,2,0:T(1,128)}, u32[]{:S(2)}) copy-start(s32[1,128,1]{1,2,0:T(1,128)} %param.13) | copy-start | bytes 1540
  362.1 43.2 %all-to-all-start.4 = ((bf16[16,24,3584]{2,1,0:T(8,128)(2,1)}), bf16[16,24,3584]{2,1,0:T(8,128)(2,1)}, u32[]{:S(2)}, u32[]{:S(2)}) async-start(bf16[16,24,3584]{2,1,0:T(8,128)(2,1)} %bitcast.153), calls=%async_computation.4 | async-start | bytes 5505024 | tf_op jit(solution)/shard_map/all_to_all | solution.py:68
  378.7 257.7 %collective-permute-start = (bf16[1,128,3584]{2,1,0:T(8,128)(2,1)}, bf16[1,128,3584]{2,1,0:T(8,128)(2,1)}, u32[]{:S(2)}, u32[]{:S(2)}) collective-permute-start(bf16[1,128,3584]{2,1,0:T(8,128)(2,1)} %fusion.27), channel_id=1, source_target_pairs={{0,32},{32,64},{64,96},{96,128},{128,160},{160,192},{192,224},{224... | collective-permute-start | bytes 2752520 | tf_op jit(solution)/shard_map/ppermute | solution.py:13
  411.8 224.6 %collective-permute-start.1 = (bf16[1,128,3584]{2,1,0:T(8,128)(2,1)S(1)}, bf16[1,128,3584]{2,1,0:T(8,128)(2,1)S(1)}, u32[]{:S(2)}, u32[]{:S(2)}) collective-permute-start(bf16[1,128,3584]{2,1,0:T(8,128)(2,1)S(1)} %fusion.28), channel_id=1, source_target_pairs={{0,224},{32,0},{64,32},{96,64},{128,96},{160,128},{192,160},{224,1... | collective-permute-start | bytes 2752520 | tf_op jit(solution)/shard_map/ppermute | solution.py:13
Sparse Core Ops, SparseCore 0:
  9.8 103.1 all-gather.3
  114.9 96.3 all-gather.7
  213.1 96.3 all-gather.5
where the time goes:
time: 650 us; the launch traced here: 646 us
  waiting for transfers between devices  296 us (46%)
  blocking collectives  224 us (34%)
  starting transfers between devices  43.3 us (7%)
  matrix products  37.4 us (6%)
  other arithmetic  19.2 us (3%)
  between operations  14 us (2%)
  local copies, waits for them, and re-layouts  11.6 us (2%)
    psum x1, blocking collectives, on_device(): gain_grad = lax.psum(gain_local, ('expert', 'dp'))  224 us
    all_gather x1, waiting for transfers between devices, on_device(): lax.all_gather(w_up, 'dp', axis=2, tiled=True)  98.2 us
    all_gather x1, waiting for transfers between devices, on_device(): lax.all_gather(w_down, 'dp', axis=2, tiled=True)  92.3 us
    all_to_all x2, waiting for transfers between devices, combine_halves(): lax.all_to_all(partial_value, 'expert', split_axis=0, concat_axis=0, tile...  38.9 us
    all_to_all x1, waiting for transfers between devices, on_device(): lax.all_to_all(fwd_buffer, 'expert', split_axis=0, concat_axis=0, tiled=T...  34 us
    all_to_all x1, waiting for transfers between devices, on_device(): lax.all_to_all(bwd_cot_buffer, 'expert', split_axis=0, concat_axis=0, til...  30.5 us
    all_to_all x2, starting transfers between devices, combine_halves(): lax.all_to_all(partial_value, 'expert', split_axis=0, concat_axis=0, tile...  16.6 us
  transfers between devices with their start and end apart: 10, of which 6 were waited for; matrix products, arithmetic and copies ran while one was open for 10% of the time, Pallas kernels for 0%

commit v1 on v0

v1 whole, which is shorter than its diff:
```python
import functools
import jax
import jax.numpy as jnp
from jax import lax
from jax.experimental import pallas as pl
from jax.experimental.pallas import tpu as pltpu
from jax.sharding import PartitionSpec as P

EPS = 1e-06
GATE_SCALE = 1.0 / 65536.0
MESH = pl.DeviceIdType.MESH
F32 = jnp.float32
BF16 = jnp.bfloat16
CW = 512
HW = CW // 2
AHEAD = 4
FIRST = 7
NT = (((1,), (1,)), ((), ()))


def plane_offsets(ny, nx):
    offsets = [(dy, dx) for dy in range(ny) for dx in range(nx) if (dy, dx) != (0, 0)]

    def hops(o):
        return min(o[0], ny - o[0]) + min(o[1], nx - o[1])

    ranked = sorted(offsets, key=lambda o: (hops(o), (o[0] + o[1]) % 2, o))
    front, back = ranked[: len(ranked) // 2], ranked[len(ranked) // 2 :][::-1]
    mixed = []
    while front or back:
        if back:
            mixed.append(back.pop(0))
        if front:
            mixed.append(front.pop(0))
    return mixed


def pack(rows, blocks, cap):
    cube = rows.reshape(blocks, cap, CW)
    return jnp.concatenate([cube[:, :, :HW], cube[:, :, HW:]], axis=1).astype(BF16)


def unpack(cube, blocks, cap):
    return jnp.concatenate([cube[:, :cap], cube[:, cap:]], axis=2).reshape(blocks * cap, CW)


def body(
    sizes,
    fx_in, bx_in, ct_in, froute, fgate, broute, bgate, gain_in, wg_in, wu_in, wd_in,
    fnext, bnext, gain_out,
    fx, bx, ct, wg, wu, wd,
    normed, f_st, b_st, inv_b, wcol_f,
    dsend, drecv, xa, fsend, frecv, bsend, brecv,
    act_a, act_b, hid, su_b, gp_b, agrad, gpre, upre,
    ngrad, lout, tgrad, gsend, grecv, gsend2, grecv2,
    in_sem, w_ss, w_rs, d_ss, d_rs, f_ss, f_rs, b_ss, b_rs, sh_ss, sh_rs, g_ss, g_rs,
):
    ns, ny, nx, experts, cap, tok, width, hidden = sizes
    ne = ny * nx
    slots = experts * cap
    rows = ne * cap
    chunks = width // CW
    blk = 2 * cap
    half_d = width // 2
    half_h = hidden // 2
    wrow = half_d // chunks
    s, e, d = lax.axis_index("section"), lax.axis_index("expert"), lax.axis_index("dp")
    y, x = e // nx, lax.rem(e, nx)
    offsets = plane_offsets(ny, nx)
    plane = [lax.rem(y + dy, ny) * nx + lax.rem(x + dx, nx) for dy, dx in offsets]
    replica = (s, e, 1 - d)
    after = (lax.rem(s + 1, ns), e, d)
    before = (lax.rem(s + ns - 1, ns), e, d)

    barrier = pltpu.get_barrier_semaphore()
    for dev in [(s, t, d) for t in plane] + [replica, after, before]:
        pl.semaphore_signal(barrier, inc=1, device_id=dev, device_id_type=MESH)

    own = [
        pltpu.make_async_copy(fx_in, fx, in_sem.at[0]),
        pltpu.make_async_copy(bx_in, bx, in_sem.at[1]),
        pltpu.make_async_copy(ct_in, ct, in_sem.at[2]),
        pltpu.make_async_copy(wg_in, wg.at[pl.ds(pl.multiple_of(d * half_d, half_d), half_d)], in_sem.at[3]),
        pltpu.make_async_copy(wu_in, wu.at[pl.ds(pl.multiple_of(d * half_d, half_d), half_d)], in_sem.at[4]),
        pltpu.make_async_copy(wd_in, wd.at[pl.ds(pl.multiple_of(d * half_h, half_h), half_h)], in_sem.at[5]),
    ]
    for copy in own:
        copy.start()
    pl.semaphore_wait(barrier, len(plane) + 3)

    def weight_copy(j):
        if j < 2 * chunks:
            src, dst = (wg_in, wg) if j < chunks else (wu_in, wu)
            k = j % chunks
            src = src.at[pl.ds(k * wrow, wrow)]
            dst = dst.at[pl.ds(pl.multiple_of(d * half_d + k * wrow, wrow), wrow)]
        else:
            return down_copy(j - 2 * chunks)
        return pltpu.make_async_remote_copy(
            src_ref=src, dst_ref=dst, send_sem=w_ss.at[j], recv_sem=w_rs.at[j],
            device_id=replica, device_id_type=MESH,
        )

    def down_copy(c):
        cols = pl.ds(c * CW if isinstance(c, int) else pl.multiple_of(c * CW, CW), CW)
        return pltpu.make_async_remote_copy(
            src_ref=wd_in.at[:, cols],
            dst_ref=wd.at[pl.ds(pl.multiple_of(d * half_h, half_h), half_h), cols],
            send_sem=w_ss.at[2 * chunks + c], recv_sem=w_rs.at[2 * chunks + c],
            device_id=replica, device_id_type=MESH,
        )

    for j in range(FIRST):
        weight_copy(j).start()

    tok_r = lax.broadcasted_iota(jnp.int32, (tok, tok), 0)
    tok_c = lax.broadcasted_iota(jnp.int32, (tok, tok), 1)

    def column(row_ref):
        spread = jnp.broadcast_to(row_ref[...].astype(F32), (tok, tok))
        return jnp.sum(jnp.where(tok_r == tok_c, spread, 0.0), axis=1, keepdims=True)

    def slot_matrix(route_ref):
        route = column(route_ref)
        onehot = (route == tok_c.astype(F32)).astype(F32)
        below = (tok_c < tok_r).astype(F32).astype(BF16)
        earlier = jnp.dot(below, onehot.astype(BF16), preferred_element_type=F32)
        rank = jnp.sum(earlier * onehot, axis=1, keepdims=True)
        slot = route * float(cap) + rank
        lanes = lax.broadcasted_iota(jnp.int32, (tok, 2 * tok), 1).astype(F32)
        return (slot == lanes).astype(F32)

    step = 16

    def normalize(src, keep):
        @pl.loop(0, tok // step)
        def _(i):
            r = pl.ds(pl.multiple_of(i * step, step), step)
            v = src[r, :].astype(F32)
            inverse = lax.rsqrt(jnp.mean(v * v, axis=-1, keepdims=True) + EPS)
            if keep:
                inv_b[r, :] = jnp.broadcast_to(inverse, (step, 128))
            normed[r, :] = (v * inverse * gain_in[...]).astype(BF16)

    def dispatch(item, source, spread):
        @pl.loop(0, chunks)
        def _(c):
            cols = pl.ds(pl.multiple_of(c * CW, CW), CW)
            put = jnp.dot(spread, source[:, cols], preferred_element_type=F32)[:slots]
            dsend[item, :, pl.ds(pl.multiple_of(c * blk, blk), blk), :] = pack(put, experts, cap)

        for i, t in enumerate(plane):
            pltpu.make_async_remote_copy(
                src_ref=dsend.at[item, t // 2], dst_ref=drecv.at[item, e],
                send_sem=d_ss.at[item], recv_sem=d_rs.at[item],
                device_id=(s, t, d), device_id_type=MESH,
            ).start()
        pltpu.make_async_copy(dsend.at[item, e // 2], drecv.at[item, e], d_rs.at[item]).start()

    st = slot_matrix(froute)
    f_st[...] = st.astype(BF16)
    f_s = st.T.astype(BF16)
    wcol_f[...] = jnp.broadcast_to(column(fgate) * GATE_SCALE, (tok, 128))
    own[0].wait()
    normalize(fx, False)
    dispatch(0, normed, f_s)

    st = slot_matrix(broute)
    b_st[...] = st.astype(BF16)
    b_s = st.T.astype(BF16)
    own[1].wait()
    normalize(bx, True)
    dispatch(1, normed, b_s)

    own[2].wait()
    wcol_b = column(bgate) * GATE_SCALE

    normed[...] = (ct[...].astype(F32) * wcol_b).astype(BF16)
    dispatch(2, normed, b_s)

    for copy in own[3:]:
        copy.wait()

    def wait_weights(lo, hi):
        for j in range(lo, hi):
            weight_copy(j).wait_recv()
            if FIRST <= j + AHEAD < 3 * chunks:
                weight_copy(j + AHEAD).start()

    def arrived(item):
        pltpu.make_async_copy(drecv.at[item], drecv.at[item], d_rs.at[item]).wait()

    def received(item, c):
        cube = drecv[item, :, pl.ds(pl.multiple_of(c * blk, blk), blk), :]
        return unpack(cube.astype(F32), ne, cap).astype(BF16)

    def project(item, weight, total):
        total[...] = jnp.zeros_like(total)

        @pl.loop(0, chunks)
        def _(c):
            cols = pl.ds(pl.multiple_of(c * CW, CW), CW)
            total[...] += jnp.dot(xa[item, :, cols], weight[cols, :], preferred_element_type=F32)

    def relayout(item):
        arrived(item)

        @pl.loop(0, chunks)
        def _(c):
            xa[item, :, pl.ds(pl.multiple_of(c * CW, CW), CW)] = received(item, c)

    wait_weights(0, FIRST)
    relayout(0)
    relayout(1)
    project(0, wg, act_a)
    project(1, wg, su_b)
    wait_weights(FIRST, 2 * chunks)
    project(0, wu, act_b)
    a = act_a[...]
    hid[...] = (a * jax.nn.sigmoid(a) * act_b[...]).astype(BF16)
    project(1, wu, gp_b)
    a = su_b[...]
    sg = jax.nn.sigmoid(a)
    gp_b[...] = gp_b[...] * sg * (1.0 + a * (1.0 - sg))
    su_b[...] = a * sg
    agrad[...] = jnp.zeros_like(agrad)
    relayout(2)

    def give_back(send, recv, c, send_sem, recv_sem):
        part = pl.ds(pl.multiple_of(c * blk, blk), blk)
        for t in plane:
            pltpu.make_async_remote_copy(
                src_ref=send.at[t, part], dst_ref=recv.at[e, part],
                send_sem=send_sem, recv_sem=recv_sem,
                device_id=(s, t, d), device_id_type=MESH,
            ).start()
        pltpu.make_async_copy(send.at[e, part], recv.at[e, part], recv_sem).start()

    @pl.loop(0, chunks)
    def _(c):
        cols = pl.ds(pl.multiple_of(c * CW, CW), CW)
        down_copy(c).wait_recv()

        @pl.when(c + AHEAD < chunks)
        def _():
            down_copy(c + AHEAD).start()

        out = jnp.dot(hid[...], wd[:, cols], preferred_element_type=F32)
        fsend[:, pl.ds(pl.multiple_of(c * blk, blk), blk), :] = pack(out, ne, cap)
        give_back(fsend, frecv, c, f_ss, f_rs)
        agrad[...] += lax.dot_general(xa[2, :, cols], wd[:, cols], NT, preferred_element_type=F32)

    g = agrad[...]
    upre[...] = (g * su_b[...]).astype(BF16)
    gpre[...] = (g * gp_b[...]).astype(BF16)

    @pl.loop(0, chunks)
    def _(c):
        cols = pl.ds(pl.multiple_of(c * CW, CW), CW)
        grad = lax.dot_general(gpre[...], wg[cols, :], NT, preferred_element_type=F32)
        grad = grad + lax.dot_general(upre[...], wu[cols, :], NT, preferred_element_type=F32)
        bsend[:, pl.ds(pl.multiple_of(c * blk, blk), blk), :] = pack(grad, ne, cap)
        give_back(bsend, brecv, c, b_ss, b_rs.at[c])

    def picked(recv, c, gather):
        cube = recv[:, pl.ds(pl.multiple_of(c * blk, blk), blk), :].astype(F32)
        cube = cube.reshape(experts, 2, blk, HW)
        both = (cube[:, 0] + cube[:, 1]).astype(BF16).astype(F32)
        rows_in = unpack(both, experts, cap).astype(BF16)
        return jnp.dot(gather[:, :slots], rows_in, preferred_element_type=F32)

    pltpu.make_async_copy(frecv, frecv, f_rs).wait()

    @pl.loop(0, chunks)
    def _(c):
        cols = pl.ds(pl.multiple_of(c * CW, CW), CW)
        mixed = wcol_f[:, :1] * picked(frecv, c, f_st)
        lout[:, cols] = (fx[:, cols].astype(F32) + mixed).astype(BF16)

    f_shift = pltpu.make_async_remote_copy(
        src_ref=lout, dst_ref=fnext, send_sem=sh_ss.at[0], recv_sem=sh_rs.at[0],
        device_id=after, device_id_type=MESH,
    )
    f_shift.start()

    gsend[...] = jnp.zeros_like(gsend)

    def take(c, inner):
        cols = pl.ds(pl.multiple_of(c * CW, CW), CW)
        part = pl.ds(pl.multiple_of(c * blk, blk), blk)
        pltpu.make_async_copy(brecv.at[:, part], brecv.at[:, part], b_rs.at[c]).wait()
        ng = picked(brecv, c, b_st)
        v = bx[:, cols].astype(F32)
        gsend[pl.ds(c, 1), :] = jnp.sum(ng * v * inv_b[:, :1], axis=0, keepdims=True)
        scaled = ng * gain_in[:, cols]
        ngrad[:, cols] = scaled
        return inner + jnp.sum(scaled * v, axis=1, keepdims=True)

    inner = lax.fori_loop(0, chunks, take, jnp.zeros((tok, 1), F32))
    inverse = inv_b[:, :1]
    slope = inverse * inverse * (inner / float(width))

    for i, t in enumerate(plane):
        pltpu.make_async_remote_copy(
            src_ref=gsend, dst_ref=grecv.at[e], send_sem=g_ss.at[0], recv_sem=g_rs.at[0],
            device_id=(s, t, d), device_id_type=MESH,
        ).start()
    pltpu.make_async_copy(gsend, grecv.at[e], g_rs.at[0]).start()

    @pl.loop(0, chunks)
    def _(c):
        cols = pl.ds(pl.multiple_of(c * CW, CW), CW)
        grad = inverse * (ngrad[:, cols] - bx[:, cols].astype(F32) * slope)
        tgrad[:, cols] = (ct[:, cols].astype(F32) + grad).astype(BF16)

    b_shift = pltpu.make_async_remote_copy(
        src_ref=tgrad, dst_ref=bnext, send_sem=sh_ss.at[1], recv_sem=sh_rs.at[1],
        device_id=before, device_id_type=MESH,
    )
    b_shift.start()

    pltpu.make_async_copy(grecv, grecv, g_rs.at[0]).wait()
    gsend2[...] = jnp.sum(grecv[...], axis=0)
    across = pltpu.make_async_remote_copy(
        src_ref=gsend2, dst_ref=grecv2, send_sem=g_ss.at[1], recv_sem=g_rs.at[1],
        device_id=replica, device_id_type=MESH,
    )
    across.start()
    across.wait()
    gain_out[...] = gsend2[...] + grecv2[...]

    for j in range(3 * chunks):
        weight_copy(j).wait_send()
    others = ne - 1
    for item in range(3):
        pltpu.make_async_copy(
            drecv.at[item, pl.ds(0, others)], drecv.at[item, pl.ds(0, others)], d_ss.at[item]
        ).wait()
    for buf, sem in ((fsend, f_ss), (bsend, b_ss)):
        pltpu.make_async_copy(buf.at[pl.ds(0, others)], buf.at[pl.ds(0, others)], sem).wait()
    pltpu.make_async_copy(grecv.at[pl.ds(0, others)], grecv.at[pl.ds(0, others)], g_ss.at[0]).wait()
    f_shift.wait()
    b_shift.wait()


def on_device(
    sizes,
    fwd_input, fwd_routes, fwd_gates, bwd_input, bwd_cotangent, bwd_routes, bwd_gates,
    norm_gain, w_gate, w_up, w_down,
):
    ns, ny, nx, experts, cap, tok, width, hidden = sizes
    ne = ny * nx
    rows = ne * cap
    chunks = width // CW
    blk = 2 * cap
    anywhere = pl.BlockSpec(memory_space=pl.ANY)
    vmem = pl.BlockSpec(memory_space=pltpu.VMEM)
    sem = pltpu.SemaphoreType.DMA
    scratch = [
        pltpu.VMEM((tok, width), BF16),
        pltpu.VMEM((tok, width), BF16),
        pltpu.VMEM((tok, width), BF16),
        pltpu.VMEM((width, hidden), BF16),
        pltpu.VMEM((width, hidden), BF16),
        pltpu.VMEM((hidden, width), BF16),
        pltpu.VMEM((tok, width), BF16),
        pltpu.VMEM((tok, 2 * tok), BF16),
        pltpu.VMEM((tok, 2 * tok), BF16),
        pltpu.VMEM((tok, 128), F32),
        pltpu.VMEM((tok, 128), F32),
        pltpu.VMEM((3, experts, chunks * blk, HW), BF16),
        pltpu.VMEM((3, ne, chunks * blk, HW), BF16),
        pltpu.VMEM((3, rows, width), BF16),
        pltpu.VMEM((ne, chunks * blk, HW), BF16),
        pltpu.VMEM((ne, chunks * blk, HW), BF16),
        pltpu.VMEM((ne, chunks * blk, HW), BF16),
        pltpu.VMEM((ne, chunks * blk, HW), BF16),
        pltpu.VMEM((rows, hidden), F32),
        pltpu.VMEM((rows, hidden), F32),
        pltpu.VMEM((rows, hidden), BF16),
        pltpu.VMEM((rows, hidden), F32),
        pltpu.VMEM((rows, hidden), F32),
        pltpu.VMEM((rows, hidden), F32),
        pltpu.VMEM((rows, hidden), BF16),
        pltpu.VMEM((rows, hidden), BF16),
        pltpu.VMEM((tok, width), F32),
        pltpu.VMEM((tok, width), BF16),
        pltpu.VMEM((tok, width), BF16),
        pltpu.VMEM((8, CW), F32),
        pltpu.VMEM((ne, 8, CW), F32),
        pltpu.VMEM((8, CW), F32),
        pltpu.VMEM((8, CW), F32),
        sem((6,)),
        sem((3 * chunks,)),
        sem((3 * chunks,)),
        sem((3,)),
        sem((3,)),
        sem,
        sem,
        sem,
        sem((chunks,)),
        sem((2,)),
        sem((2,)),
        sem((2,)),
        sem((2,)),
    ]
    fnext, bnext, gain = pl.pallas_call(
        functools.partial(body, sizes),
        out_shape=[
            jax.ShapeDtypeStruct((tok, width), BF16),
            jax.ShapeDtypeStruct((tok, width), BF16),
            jax.ShapeDtypeStruct((8, CW), F32),
        ],
        in_specs=[anywhere] * 3 + [vmem] * 5 + [anywhere] * 3,
        out_specs=[anywhere, anywhere, vmem],
        scratch_shapes=scratch,
        compiler_params=pltpu.CompilerParams(
            collective_id=0, has_side_effects=True, vmem_limit_bytes=62 * 2**20
        ),
    )(
        fwd_input[0], bwd_input[0], bwd_cotangent[0],
        fwd_routes.reshape(1, tok), fwd_gates.reshape(1, tok),
        bwd_routes.reshape(1, tok), bwd_gates.reshape(1, tok),
        norm_gain, w_gate[0, 0], w_up[0, 0], w_down[0, 0],
    )
    return fnext[None], bnext[None], gain[:chunks].reshape(1, width)


def solution(mesh):
    ns, ne, ndp = mesh.shape["section"], mesh.shape["expert"], mesh.shape["dp"]
    ny = 4 if ne == 16 else 2
    sizes = (ns, ny, ne // ny, ne // 2, 24, 128, 3584, 512)
    tokens = P("section", ("expert", "dp"), None)
    return jax.shard_map(
        functools.partial(on_device, sizes),
        mesh=mesh,
        in_specs=(tokens,) * 7
        + (P("section", None),)
        + (P("section", "expert", "dp", None),) * 3,
        out_specs=(tokens, tokens, P("section", None)),
        check_vma=False,
    )
```

time: 650 us -> 309 us (0.48)
  Pallas kernels: 0 us -> 304 us
  waiting for transfers between devices: 296 us -> 0 us
  blocking collectives: 224 us -> 0 us
  starting transfers between devices: 43.3 us -> 0 us
  matrix products: 37.4 us -> 0 us
  other arithmetic: 19.2 us -> 0 us
  between operations: 14 us -> 0.65 us
  local copies, waits for them, and re-layouts: 11.6 us -> 4.5 us
    pallas_call x0 -> x1, Pallas kernels: none -> 304 us  [on_device(): pl.pallas_call(functools.partial(body, sizes), out_shape=[jax.ShapeDtypeS...]
    psum x1 -> x0, blocking collectives: 224 us -> none  [on_device(): gain_grad = lax.psum(gain_local, ('expert', 'dp'))]
    all_gather x3 -> x0, waiting for transfers between devices: 191 us -> none  [the longest x1 98.2 us: on_device(): lax.all_gather(w_up, 'dp', axis=2, tiled=True)]
    all_to_all x5 -> x0, waiting for transfers between devices: 103 us -> none  [the longest x2 38.9 us: combine_halves(): lax.all_to_all(partial_value, 'expert', split_axis=0, concat_axis=0, tile...]
    all_to_all x5 -> x0, starting transfers between devices: 43.1 us -> none  [the longest x2 16.6 us: combine_halves(): lax.all_to_all(partial_value, 'expert', split_axis=0, concat_axis=0, tile...]
    dot_general x6 -> x0, matrix products: 37.4 us -> none  [the longest x1 9.54 us: expert_backward(): lax.dot_general(gate_pre, gate_mat, last_dims, preferred_element_type=jnp...]
    convert_element_type x8 -> x0, other arithmetic: 9.92 us -> none  [the longest x2 4.9 us: combine_halves(): both = back.reshape(experts, 2, 2 * half_cap, width).astype(jnp.float32)]
    scatter x3 -> x0, other arithmetic: 7.18 us -> none  [place_rows(): jnp.zeros((experts * capacity, width), row_data.dtype).at[slot_index]]
  transfers between devices with their start and end apart: 10 -> 0, of which waited for: 6 -> 0; matrix products, arithmetic and copies ran while one was open for 10% -> 0% of each run, Pallas kernels for 0% -> 0%
where the time goes in v1:
time: 309 us
  Pallas kernels  304 us (98%)
  local copies, waits for them, and re-layouts  4.5 us (1%)
    pallas_call x1, Pallas kernels, on_device(): pl.pallas_call(functools.partial(body, sizes), out_shape=[jax.ShapeDtypeS...  304 us

profile of v1, /device:TPU:2, one launch (start us, length us, event | category | flops | bytes accessed | tf_op | source)
XLA Modules:
  0.0 308.9 jit_solution(4574434028870359989)
XLA Ops:
  0.6 303.7 %shard_map.130 = (bf16[128,3584]{1,0:T(8,128)(2,1)}, bf16[128,3584]{1,0:T(8,128)(2,1)}, f32[8,512]{1,0:T(8,128)}) custom-call(bf16[128,3584]{1,0:T(8,128)(2,1)} %bitcast.21, bf16[128,3584]{1,0:T(8,128)(2,1)} %bitcast.22, bf16[128,3584]{1,0:T(8,128)(2,1)} %bitcast.23, s32[1,128]{1,0:T(1,128)} %bitcast.25, s32[1,128]{1,0:T(1,128)} %bitcast.26, ...), custom_call_target="tpu_custom_call" | custom-call | tf_op jit(solution)/shard_map/pallas_call | solution.py:407
  304.4 0.0 copy-start
  304.4 0.8 slice_bitcast_fusion
  305.2 0.6 copy.14
  305.8 2.2 copy.17
  308.0 0.0 copy-done
  308.0 0.9 copy.18
Async XLA Ops:
  304.4 3.6 %copy-start = (bf16[128,3584]{1,0:T(8,128)(2,1)S(1)}, bf16[128,3584]{1,0:T(8,128)(2,1)}, u32[]{:S(2)}) copy-start(bf16[128,3584]{1,0:T(8,128)(2,1)} %get-tuple-element.7) | copy-start | bytes 2752516

commit v2 on v1

--- a/solution.py
+++ b/solution.py
@@ -49,11 +49,11 @@
     fx_in, bx_in, ct_in, froute, fgate, broute, bgate, gain_in, wg_in, wu_in, wd_in,
     fnext, bnext, gain_out,
     fx, bx, ct, wg, wu, wd,
-    normed, f_st, b_st, inv_b, wcol_f,
+    normed, f_st, b_st, b_oe, b_rk, inv_b, wcol_f,
     dsend, drecv, xa, fsend, frecv, bsend, brecv,
     act_a, act_b, hid, su_b, gp_b, agrad, gpre, upre,
-    ngrad, lout, tgrad, gsend, grecv, gsend2, grecv2,
-    in_sem, w_ss, w_rs, d_ss, d_rs, f_ss, f_rs, b_ss, b_rs, sh_ss, sh_rs, g_ss, g_rs,
+    lout, tgrad, isend, irecv, gsend, grecv, gsend2, grecv2,
+    in_sem, w_ss, w_rs, d_ss, d_rs, f_ss, f_rs, b_ss, b_rs, sh_ss, sh_rs, t_ss, t_rs, i_ss, i_rs, g_ss, g_rs,
 ):
     ns, ny, nx, experts, cap, tok, width, hidden = sizes
     ne = ny * nx
@@ -128,7 +128,7 @@
         rank = jnp.sum(earlier * onehot, axis=1, keepdims=True)
         slot = route * float(cap) + rank
         lanes = lax.broadcasted_iota(jnp.int32, (tok, 2 * tok), 1).astype(F32)
-        return (slot == lanes).astype(F32)
+        return (slot == lanes).astype(F32), onehot, (rank == tok_c.astype(F32)).astype(F32)
 
     step = 16
 
@@ -157,7 +157,7 @@
             ).start()
         pltpu.make_async_copy(dsend.at[item, e // 2], drecv.at[item, e], d_rs.at[item]).start()
 
-    st = slot_matrix(froute)
+    st, _, _ = slot_matrix(froute)
     f_st[...] = st.astype(BF16)
     f_s = st.T.astype(BF16)
     wcol_f[...] = jnp.broadcast_to(column(fgate) * GATE_SCALE, (tok, 128))
@@ -165,7 +165,7 @@
     normalize(fx, False)
     dispatch(0, normed, f_s)
 
-    st = slot_matrix(broute)
+    st, b_oe[...], b_rk[...] = slot_matrix(broute)
     b_st[...] = st.astype(BF16)
     b_s = st.T.astype(BF16)
     own[1].wait()
@@ -221,8 +221,11 @@
     project(1, wu, gp_b)
     a = su_b[...]
     sg = jax.nn.sigmoid(a)
-    gp_b[...] = gp_b[...] * sg * (1.0 + a * (1.0 - sg))
+    b = gp_b[...]
+    gp = b * sg * (1.0 + a * (1.0 - sg))
+    gp_b[...] = gp
     su_b[...] = a * sg
+    act_a[...] = a * gp + b * (a * sg)
     agrad[...] = jnp.zeros_like(agrad)
     relayout(2)
 
@@ -236,6 +239,13 @@
             ).start()
         pltpu.make_async_copy(send.at[e, part], recv.at[e, part], recv_sem).start()
 
+    def forward_chunk(c):
+        cols = pl.ds(c * CW if isinstance(c, int) else pl.multiple_of(c * CW, CW), CW)
+        out = jnp.dot(hid[...], wd[:, cols], preferred_element_type=F32)
+        part = pl.ds(c * blk if isinstance(c, int) else pl.multiple_of(c * blk, blk), blk)
+        fsend[:, part, :] = pack(out, ne, cap)
+        give_back(fsend, frecv, c, f_ss, f_rs)
+
     @pl.loop(0, chunks)
     def _(c):
         cols = pl.ds(pl.multiple_of(c * CW, CW), CW)
@@ -245,14 +255,29 @@
         def _():
             down_copy(c + AHEAD).start()
 
-        out = jnp.dot(hid[...], wd[:, cols], preferred_element_type=F32)
-        fsend[:, pl.ds(pl.multiple_of(c * blk, blk), blk), :] = pack(out, ne, cap)
-        give_back(fsend, frecv, c, f_ss, f_rs)
         agrad[...] += lax.dot_general(xa[2, :, cols], wd[:, cols], NT, preferred_element_type=F32)
+
+        @pl.when(c < chunks - 1)
+        def _():
+            forward_chunk(c)
 
     g = agrad[...]
     upre[...] = (g * su_b[...]).astype(BF16)
     gpre[...] = (g * gp_b[...]).astype(BF16)
+
+    dots = jnp.sum(g * act_a[...], axis=1, keepdims=True)
+    dots = jnp.broadcast_to(dots, (rows, 128)).reshape(ne, cap, 128)
+    place = lax.broadcasted_iota(jnp.int32, (ne, cap, 128), 1)
+    lane = lax.broadcasted_iota(jnp.int32, (ne, cap, 128), 2)
+    dots = jnp.sum(jnp.where(place == lane, dots, 0.0), axis=1, keepdims=True)
+    isend[...] = jnp.broadcast_to(dots, (ne, 8, 128))
+    for t in plane:
+        pltpu.make_async_remote_copy(
+            src_ref=isend.at[t], dst_ref=irecv.at[e], send_sem=i_ss, recv_sem=i_rs,
+            device_id=(s, t, d), device_id_type=MESH,
+        ).start()
+    pltpu.make_async_copy(isend.at[e], irecv.at[e], i_rs).start()
+    gsend[...] = jnp.zeros_like(gsend)
 
     @pl.loop(0, chunks)
     def _(c):
@@ -261,6 +286,19 @@
         grad = grad + lax.dot_general(upre[...], wu[cols, :], NT, preferred_element_type=F32)
         bsend[:, pl.ds(pl.multiple_of(c * blk, blk), blk), :] = pack(grad, ne, cap)
         give_back(bsend, brecv, c, b_ss, b_rs.at[c])
+        total = jnp.sum(grad * xa[1, :, cols].astype(F32), axis=0, keepdims=True)
+        gsend[pl.ds(c, 1), :] = total / gain_in[:, cols]
+
+        @pl.when(c == 0)
+        def _():
+            forward_chunk(chunks - 1)
+
+    for t in plane:
+        pltpu.make_async_remote_copy(
+            src_ref=gsend, dst_ref=grecv.at[e], send_sem=g_ss.at[0], recv_sem=g_rs.at[0],
+            device_id=(s, t, d), device_id_type=MESH,
+        ).start()
+    pltpu.make_async_copy(gsend, grecv.at[e], g_rs.at[0]).start()
 
     def picked(recv, c, gather):
         cube = recv[:, pl.ds(pl.multiple_of(c * blk, blk), blk), :].astype(F32)
@@ -278,46 +316,39 @@
         lout[:, cols] = (fx[:, cols].astype(F32) + mixed).astype(BF16)
 
     f_shift = pltpu.make_async_remote_copy(
-        src_ref=lout, dst_ref=fnext, send_sem=sh_ss.at[0], recv_sem=sh_rs.at[0],
+        src_ref=lout, dst_ref=fnext, send_sem=sh_ss, recv_sem=sh_rs,
         device_id=after, device_id_type=MESH,
     )
     f_shift.start()
 
-    gsend[...] = jnp.zeros_like(gsend)
-
-    def take(c, inner):
+    pltpu.make_async_copy(irecv, irecv, i_rs).wait()
+    per_expert = jnp.sum(irecv[...].reshape(experts, 2, 8, 128), axis=1)
+    spread = jnp.zeros((tok, 128), F32)
+    for k in range(experts):
+        spread = spread + b_oe[:, k : k + 1] * per_expert[k, :1, :]
+    inverse = inv_b[:, :1]
+    slope = inverse * jnp.sum(spread * b_rk[...], axis=1, keepdims=True) * (1.0 / width)
+    inv_b[...] = jnp.broadcast_to(inverse, (tok, 128))
+    b_rk[...] = jnp.broadcast_to(inverse * slope, (tok, 128))
+
+    def shift_chunk(c):
+        cols = pl.ds(c * CW if isinstance(c, int) else pl.multiple_of(c * CW, CW), CW)
+        return pltpu.make_async_remote_copy(
+            src_ref=tgrad.at[:, cols], dst_ref=bnext.at[:, cols],
+            send_sem=t_ss.at[c], recv_sem=t_rs.at[c],
+            device_id=before, device_id_type=MESH,
+        )
+
+    def take(c):
         cols = pl.ds(pl.multiple_of(c * CW, CW), CW)
         part = pl.ds(pl.multiple_of(c * blk, blk), blk)
         pltpu.make_async_copy(brecv.at[:, part], brecv.at[:, part], b_rs.at[c]).wait()
-        ng = picked(brecv, c, b_st)
-        v = bx[:, cols].astype(F32)
-        gsend[pl.ds(c, 1), :] = jnp.sum(ng * v * inv_b[:, :1], axis=0, keepdims=True)
-        scaled = ng * gain_in[:, cols]
-        ngrad[:, cols] = scaled
-        return inner + jnp.sum(scaled * v, axis=1, keepdims=True)
-
-    inner = lax.fori_loop(0, chunks, take, jnp.zeros((tok, 1), F32))
-    inverse = inv_b[:, :1]
-    slope = inverse * inverse * (inner / float(width))
-
-    for i, t in enumerate(plane):
-        pltpu.make_async_remote_copy(
-            src_ref=gsend, dst_ref=grecv.at[e], send_sem=g_ss.at[0], recv_sem=g_rs.at[0],
-            device_id=(s, t, d), device_id_type=MESH,
-        ).start()
-    pltpu.make_async_copy(gsend, grecv.at[e], g_rs.at[0]).start()
-
-    @pl.loop(0, chunks)
-    def _(c):
-        cols = pl.ds(pl.multiple_of(c * CW, CW), CW)
-        grad = inverse * (ngrad[:, cols] - bx[:, cols].astype(F32) * slope)
+        scaled = picked(brecv, c, b_st) * gain_in[:, cols]
+        grad = inv_b[:, :1] * scaled - bx[:, cols].astype(F32) * b_rk[:, :1]
         tgrad[:, cols] = (ct[:, cols].astype(F32) + grad).astype(BF16)
-
-    b_shift = pltpu.make_async_remote_copy(
-        src_ref=tgrad, dst_ref=bnext, send_sem=sh_ss.at[1], recv_sem=sh_rs.at[1],
-        device_id=before, device_id_type=MESH,
-    )
-    b_shift.start()
+        shift_chunk(c).start()
+
+    pl.loop(0, chunks - 1)(take)
 
     pltpu.make_async_copy(grecv, grecv, g_rs.at[0]).wait()
     gsend2[...] = jnp.sum(grecv[...], axis=0)
@@ -326,8 +357,10 @@
         device_id=replica, device_id_type=MESH,
     )
     across.start()
+    take(chunks - 1)
     across.wait()
-    gain_out[...] = gsend2[...] + grecv2[...]
+    for c in range(chunks):
+        gain_out[:, c * CW : (c + 1) * CW] = gsend2[c : c + 1, :] + grecv2[c : c + 1, :]
 
     for j in range(3 * chunks):
         weight_copy(j).wait_send()
@@ -339,8 +372,10 @@
     for buf, sem in ((fsend, f_ss), (bsend, b_ss)):
         pltpu.make_async_copy(buf.at[pl.ds(0, others)], buf.at[pl.ds(0, others)], sem).wait()
     pltpu.make_async_copy(grecv.at[pl.ds(0, others)], grecv.at[pl.ds(0, others)], g_ss.at[0]).wait()
+    pltpu.make_async_copy(isend.at[pl.ds(0, others)], isend.at[pl.ds(0, others)], i_ss).wait()
     f_shift.wait()
-    b_shift.wait()
+    for c in range(chunks):
+        shift_chunk(c).wait()
 
 
 def on_device(
@@ -366,6 +401,8 @@
         pltpu.VMEM((tok, width), BF16),
         pltpu.VMEM((tok, 2 * tok), BF16),
         pltpu.VMEM((tok, 2 * tok), BF16),
+        pltpu.VMEM((tok, 128), F32),
+        pltpu.VMEM((tok, 128), F32),
         pltpu.VMEM((tok, 128), F32),
         pltpu.VMEM((tok, 128), F32),
         pltpu.VMEM((3, experts, chunks * blk, HW), BF16),
@@ -383,9 +420,10 @@
         pltpu.VMEM((rows, hidden), F32),
         pltpu.VMEM((rows, hidden), BF16),
         pltpu.VMEM((rows, hidden), BF16),
-        pltpu.VMEM((tok, width), F32),
-        pltpu.VMEM((tok, width), BF16),
-        pltpu.VMEM((tok, width), BF16),
+        pltpu.VMEM((tok, width), BF16),
+        pltpu.VMEM((tok, width), BF16),
+        pltpu.VMEM((ne, 8, 128), F32),
+        pltpu.VMEM((ne, 8, 128), F32),
         pltpu.VMEM((8, CW), F32),
         pltpu.VMEM((ne, 8, CW), F32),
         pltpu.VMEM((8, CW), F32),
@@ -399,8 +437,12 @@
         sem,
         sem,
         sem((chunks,)),
-        sem((2,)),
-        sem((2,)),
+        sem,
+        sem,
+        sem((chunks,)),
+        sem((chunks,)),
+        sem,
+        sem,
         sem((2,)),
         sem((2,)),
     ]
@@ -409,7 +451,7 @@
         out_shape=[
             jax.ShapeDtypeStruct((tok, width), BF16),
             jax.ShapeDtypeStruct((tok, width), BF16),
-            jax.ShapeDtypeStruct((8, CW), F32),
+            jax.ShapeDtypeStruct((1, width), F32),
         ],
         in_specs=[anywhere] * 3 + [vmem] * 5 + [anywhere] * 3,
         out_specs=[anywhere, anywhere, vmem],
@@ -423,7 +465,7 @@
         bwd_routes.reshape(1, tok), bwd_gates.reshape(1, tok),
         norm_gain, w_gate[0, 0], w_up[0, 0], w_down[0, 0],
     )
-    return fnext[None], bnext[None], gain[:chunks].reshape(1, width)
+    return fnext[None], bnext[None], gain
 
 
 def solution(mesh):

time: 309 us -> 301 us (0.974)
  Pallas kernels: 304 us -> 297 us
    pallas_call x1, Pallas kernels: 304 us -> 297 us  [on_device(): pl.pallas_call(functools.partial(body, sizes), out_shape=[jax.ShapeDtypeS...]
where the time goes in v2:
time: 301 us
  Pallas kernels  297 us (99%)
  local copies, waits for them, and re-layouts  3.77 us (1%)
    pallas_call x1, Pallas kernels, on_device(): pl.pallas_call(functools.partial(body, sizes), out_shape=[jax.ShapeDtypeS...  297 us

profile of v2, /device:TPU:2, one launch (start us, length us, event | category | flops | bytes accessed | tf_op | source)
XLA Modules:
  0.0 301.2 jit_solution(1589266430678528268)
XLA Ops:
  0.6 296.7 %shard_map.130 = (bf16[128,3584]{1,0:T(8,128)(2,1)}, bf16[128,3584]{1,0:T(8,128)(2,1)}, f32[1,3584]{1,0:T(1,128)}) custom-call(bf16[128,3584]{1,0:T(8,128)(2,1)} %bitcast.17, bf16[128,3584]{1,0:T(8,128)(2,1)} %bitcast.18, bf16[128,3584]{1,0:T(8,128)(2,1)} %bitcast.19, s32[1,128]{1,0:T(1,128)} %bitcast.20, s32[1,128]{1,0:T(1,128)} %bitcast.21, ...), custom_call_target="tpu_custom_call" | custom-call | tf_op jit(solution)/shard_map/pallas_call | solution.py:449
  297.4 0.0 copy-start
  297.4 0.0 copy-start.1
  297.4 2.2 copy.17
  299.6 0.0 copy-done
  299.6 0.9 copy.18
  300.6 0.0 copy-done.1
  300.6 0.6 copy.19
Async XLA Ops:
  297.4 2.3 copy-start
  297.4 3.2 %copy-start.1 = (f32[1,3584]{1,0:T(1,128)S(1)}, f32[1,3584]{1,0:T(1,128)}, u32[]{:S(2)}) copy-start(f32[1,3584]{1,0:T(1,128)} %get-tuple-element.14) | copy-start | bytes 43012

commit v3 on v2

--- a/solution.py
+++ b/solution.py
@@ -11,10 +11,10 @@
 MESH = pl.DeviceIdType.MESH
 F32 = jnp.float32
 BF16 = jnp.bfloat16
-CW = 512
+CW = 256
 HW = CW // 2
-AHEAD = 4
-FIRST = 7
+AHEAD = 14
+FIRST = 28
 NT = (((1,), (1,)), ((), ()))
 
 
@@ -52,7 +52,7 @@
     normed, f_st, b_st, b_oe, b_rk, inv_b, wcol_f,
     dsend, drecv, xa, fsend, frecv, bsend, brecv,
     act_a, act_b, hid, su_b, gp_b, agrad, gpre, upre,
-    lout, tgrad, isend, irecv, gsend, grecv, gsend2, grecv2,
+    lout, tgrad, isend, irecv, gsend, gsend2, grecv, grecv2,
     in_sem, w_ss, w_rs, d_ss, d_rs, f_ss, f_rs, b_ss, b_rs, sh_ss, sh_rs, t_ss, t_rs, i_ss, i_rs, g_ss, g_rs,
 ):
     ns, ny, nx, experts, cap, tok, width, hidden = sizes
@@ -82,8 +82,12 @@
         pltpu.make_async_copy(ct_in, ct, in_sem.at[2]),
         pltpu.make_async_copy(wg_in, wg.at[pl.ds(pl.multiple_of(d * half_d, half_d), half_d)], in_sem.at[3]),
         pltpu.make_async_copy(wu_in, wu.at[pl.ds(pl.multiple_of(d * half_d, half_d), half_d)], in_sem.at[4]),
-        pltpu.make_async_copy(wd_in, wd.at[pl.ds(pl.multiple_of(d * half_h, half_h), half_h)], in_sem.at[5]),
     ]
+    own_rows = pl.ds(pl.multiple_of(d * half_h, half_h), half_h)
+    for c in range(chunks):
+        pltpu.make_async_copy(
+            wd_in.at[:, pl.ds(c * CW, CW)], wd.at[c, own_rows], in_sem.at[5]
+        ).start()
     for copy in own:
         copy.start()
     pl.semaphore_wait(barrier, len(plane) + 3)
@@ -102,10 +106,9 @@
         )
 
     def down_copy(c):
-        cols = pl.ds(c * CW if isinstance(c, int) else pl.multiple_of(c * CW, CW), CW)
         return pltpu.make_async_remote_copy(
-            src_ref=wd_in.at[:, cols],
-            dst_ref=wd.at[pl.ds(pl.multiple_of(d * half_h, half_h), half_h), cols],
+            src_ref=wd.at[c, own_rows],
+            dst_ref=wd.at[c, own_rows],
             send_sem=w_ss.at[2 * chunks + c], recv_sem=w_rs.at[2 * chunks + c],
             device_id=replica, device_id_type=MESH,
         )
@@ -180,6 +183,7 @@
 
     for copy in own[3:]:
         copy.wait()
+    pltpu.make_async_copy(wd.at[:, own_rows], wd.at[:, own_rows], in_sem.at[5]).wait()
 
     def wait_weights(lo, hi):
         for j in range(lo, hi):
@@ -209,12 +213,12 @@
         def _(c):
             xa[item, :, pl.ds(pl.multiple_of(c * CW, CW), CW)] = received(item, c)
 
-    wait_weights(0, FIRST)
+    wait_weights(0, chunks)
     relayout(0)
     relayout(1)
     project(0, wg, act_a)
     project(1, wg, su_b)
-    wait_weights(FIRST, 2 * chunks)
+    wait_weights(chunks, 2 * chunks)
     project(0, wu, act_b)
     a = act_a[...]
     hid[...] = (a * jax.nn.sigmoid(a) * act_b[...]).astype(BF16)
@@ -240,8 +244,7 @@
         pltpu.make_async_copy(send.at[e, part], recv.at[e, part], recv_sem).start()
 
     def forward_chunk(c):
-        cols = pl.ds(c * CW if isinstance(c, int) else pl.multiple_of(c * CW, CW), CW)
-        out = jnp.dot(hid[...], wd[:, cols], preferred_element_type=F32)
+        out = jnp.dot(hid[...], wd[c], preferred_element_type=F32)
         part = pl.ds(c * blk if isinstance(c, int) else pl.multiple_of(c * blk, blk), blk)
         fsend[:, part, :] = pack(out, ne, cap)
         give_back(fsend, frecv, c, f_ss, f_rs)
@@ -255,7 +258,7 @@
         def _():
             down_copy(c + AHEAD).start()
 
-        agrad[...] += lax.dot_general(xa[2, :, cols], wd[:, cols], NT, preferred_element_type=F32)
+        agrad[...] += lax.dot_general(xa[2, :, cols], wd[c], NT, preferred_element_type=F32)
 
         @pl.when(c < chunks - 1)
         def _():
@@ -279,26 +282,36 @@
     pltpu.make_async_copy(isend.at[e], irecv.at[e], i_rs).start()
     gsend[...] = jnp.zeros_like(gsend)
 
-    @pl.loop(0, chunks)
-    def _(c):
+    def backward_chunk(c):
         cols = pl.ds(pl.multiple_of(c * CW, CW), CW)
         grad = lax.dot_general(gpre[...], wg[cols, :], NT, preferred_element_type=F32)
         grad = grad + lax.dot_general(upre[...], wu[cols, :], NT, preferred_element_type=F32)
         bsend[:, pl.ds(pl.multiple_of(c * blk, blk), blk), :] = pack(grad, ne, cap)
-        give_back(bsend, brecv, c, b_ss, b_rs.at[c])
         total = jnp.sum(grad * xa[1, :, cols].astype(F32), axis=0, keepdims=True)
         gsend[pl.ds(c, 1), :] = total / gain_in[:, cols]
 
-        @pl.when(c == 0)
+    def backward_send(c):
+        give_back(bsend, brecv, c, b_ss, b_rs.at[c])
+
+    held = chunks * 9 // 14
+
+    @pl.loop(0, held)
+    def _(c):
+        backward_chunk(c)
+        backward_send(c)
+
+        @pl.when(c == 1)
         def _():
             forward_chunk(chunks - 1)
 
+    pl.loop(held, chunks)(backward_chunk)
     for t in plane:
         pltpu.make_async_remote_copy(
             src_ref=gsend, dst_ref=grecv.at[e], send_sem=g_ss.at[0], recv_sem=g_rs.at[0],
             device_id=(s, t, d), device_id_type=MESH,
         ).start()
     pltpu.make_async_copy(gsend, grecv.at[e], g_rs.at[0]).start()
+    pl.loop(held, chunks)(backward_send)
 
     def picked(recv, c, gather):
         cube = recv[:, pl.ds(pl.multiple_of(c * blk, blk), blk), :].astype(F32)
@@ -348,7 +361,7 @@
         tgrad[:, cols] = (ct[:, cols].astype(F32) + grad).astype(BF16)
         shift_chunk(c).start()
 
-    pl.loop(0, chunks - 1)(take)
+    pl.loop(0, held)(take)
 
     pltpu.make_async_copy(grecv, grecv, g_rs.at[0]).wait()
     gsend2[...] = jnp.sum(grecv[...], axis=0)
@@ -357,7 +370,7 @@
         device_id=replica, device_id_type=MESH,
     )
     across.start()
-    take(chunks - 1)
+    pl.loop(held, chunks)(take)
     across.wait()
     for c in range(chunks):
         gain_out[:, c * CW : (c + 1) * CW] = gsend2[c : c + 1, :] + grecv2[c : c + 1, :]
@@ -397,7 +410,7 @@
         pltpu.VMEM((tok, width), BF16),
         pltpu.VMEM((width, hidden), BF16),
         pltpu.VMEM((width, hidden), BF16),
-        pltpu.VMEM((hidden, width), BF16),
+        pltpu.VMEM((chunks, hidden, CW), BF16),
         pltpu.VMEM((tok, width), BF16),
         pltpu.VMEM((tok, 2 * tok), BF16),
         pltpu.VMEM((tok, 2 * tok), BF16),
@@ -424,10 +437,10 @@
         pltpu.VMEM((tok, width), BF16),
         pltpu.VMEM((ne, 8, 128), F32),
         pltpu.VMEM((ne, 8, 128), F32),
-        pltpu.VMEM((8, CW), F32),
-        pltpu.VMEM((ne, 8, CW), F32),
-        pltpu.VMEM((8, CW), F32),
-        pltpu.VMEM((8, CW), F32),
+        pltpu.VMEM((16, CW), F32),
+        pltpu.VMEM((16, CW), F32),
+        pltpu.VMEM((ne, 16, CW), F32),
+        pltpu.VMEM((16, CW), F32),
         sem((6,)),
         sem((3 * chunks,)),
         sem((3 * chunks,)),

time: 301 us -> 297 us (0.987)
  Pallas kernels: 297 us -> 293 us
    pallas_call x1, Pallas kernels: 297 us -> 293 us  [on_device(): pl.pallas_call(functools.partial(body, sizes), out_shape=[jax.ShapeDtypeS...]
where the time goes in v3:
time: 297 us
  Pallas kernels  293 us (99%)
  local copies, waits for them, and re-layouts  3.77 us (1%)
    pallas_call x1, Pallas kernels, on_device(): pl.pallas_call(functools.partial(body, sizes), out_shape=[jax.ShapeDtypeS...  293 us

profile of v3, /device:TPU:2, one launch (start us, length us, event | category | flops | bytes accessed | tf_op | source)
XLA Modules:
  0.0 297.2 jit_solution(17118936989175774469)
XLA Ops:
  0.6 292.8 %shard_map.130 = (bf16[128,3584]{1,0:T(8,128)(2,1)}, bf16[128,3584]{1,0:T(8,128)(2,1)}, f32[1,3584]{1,0:T(1,128)}) custom-call(bf16[128,3584]{1,0:T(8,128)(2,1)} %bitcast.17, bf16[128,3584]{1,0:T(8,128)(2,1)} %bitcast.18, bf16[128,3584]{1,0:T(8,128)(2,1)} %bitcast.19, s32[1,128]{1,0:T(1,128)} %bitcast.20, s32[1,128]{1,0:T(1,128)} %bitcast.21, ...), custom_call_target="tpu_custom_call" | custom-call | tf_op jit(solution)/shard_map/pallas_call | solution.py:462
  293.5 0.0 copy-start
  293.5 0.0 copy-start.1
  293.5 2.2 copy.17
  295.7 0.0 copy-done
  295.7 0.9 copy.18
  296.6 0.0 copy-done.1
  296.6 0.6 copy.19
Async XLA Ops:
  293.5 2.3 copy-start
  293.5 3.2 %copy-start.1 = (f32[1,3584]{1,0:T(1,128)S(1)}, f32[1,3584]{1,0:T(1,128)}, u32[]{:S(2)}) copy-start(f32[1,3584]{1,0:T(1,128)} %get-tuple-element.14) | copy-start | bytes 43012

commit v4 on v3

--- a/solution.py
+++ b/solution.py
@@ -15,6 +15,7 @@
 HW = CW // 2
 AHEAD = 14
 FIRST = 28
+LAG = 4
 NT = (((1,), (1,)), ((), ()))
 
 
@@ -52,7 +53,7 @@
     normed, f_st, b_st, b_oe, b_rk, inv_b, wcol_f,
     dsend, drecv, xa, fsend, frecv, bsend, brecv,
     act_a, act_b, hid, su_b, gp_b, agrad, gpre, upre,
-    lout, tgrad, isend, irecv, gsend, gsend2, grecv, grecv2,
+    lout, tgrad, isend, irecv, gsend, gsend2, gsend3, grecv, grecv2,
     in_sem, w_ss, w_rs, d_ss, d_rs, f_ss, f_rs, b_ss, b_rs, sh_ss, sh_rs, t_ss, t_rs, i_ss, i_rs, g_ss, g_rs,
 ):
     ns, ny, nx, experts, cap, tok, width, hidden = sizes
@@ -234,7 +235,7 @@
     relayout(2)
 
     def give_back(send, recv, c, send_sem, recv_sem):
-        part = pl.ds(pl.multiple_of(c * blk, blk), blk)
+        part = pl.ds(c * blk if isinstance(c, int) else pl.multiple_of(c * blk, blk), blk)
         for t in plane:
             pltpu.make_async_remote_copy(
                 src_ref=send.at[t, part], dst_ref=recv.at[e, part],
@@ -243,11 +244,35 @@
             ).start()
         pltpu.make_async_copy(send.at[e, part], recv.at[e, part], recv_sem).start()
 
+    def picked(recv, c, gather):
+        cube = recv[:, pl.ds(pl.multiple_of(c * blk, blk), blk), :].astype(F32)
+        cube = cube.reshape(experts, 2, blk, HW)
+        both = (cube[:, 0] + cube[:, 1]).astype(BF16).astype(F32)
+        rows_in = unpack(both, experts, cap).astype(BF16)
+        return jnp.dot(gather[:, :slots], rows_in, preferred_element_type=F32)
+
+    def forward_take(c):
+        cols = pl.ds(pl.multiple_of(c * CW, CW), CW)
+        part = pl.ds(pl.multiple_of(c * blk, blk), blk)
+        pltpu.make_async_copy(frecv.at[:, part], frecv.at[:, part], f_rs.at[c]).wait()
+        mixed = wcol_f[:, :1] * picked(frecv, c, f_st)
+        lout[:, cols] = (fx[:, cols].astype(F32) + mixed).astype(BF16)
+
+    split = (chunks - LAG) * CW
+    f_shifts = [
+        pltpu.make_async_remote_copy(
+            src_ref=lout.at[:, pl.ds(start, size)], dst_ref=fnext.at[:, pl.ds(start, size)],
+            send_sem=sh_ss.at[i], recv_sem=sh_rs.at[i],
+            device_id=after, device_id_type=MESH,
+        )
+        for i, (start, size) in enumerate(((0, split), (split, width - split)))
+    ]
+
     def forward_chunk(c):
         out = jnp.dot(hid[...], wd[c], preferred_element_type=F32)
         part = pl.ds(c * blk if isinstance(c, int) else pl.multiple_of(c * blk, blk), blk)
         fsend[:, part, :] = pack(out, ne, cap)
-        give_back(fsend, frecv, c, f_ss, f_rs)
+        give_back(fsend, frecv, c, f_ss, f_rs.at[c])
 
     @pl.loop(0, chunks)
     def _(c):
@@ -264,10 +289,32 @@
         def _():
             forward_chunk(c)
 
+        @pl.when(c >= LAG)
+        def _():
+            forward_take(c - LAG)
+
+    f_shifts[0].start()
     g = agrad[...]
     upre[...] = (g * su_b[...]).astype(BF16)
     gpre[...] = (g * gp_b[...]).astype(BF16)
 
+    gsend[...] = jnp.zeros_like(gsend)
+
+    def backward_chunk(c):
+        cols = pl.ds(c * CW if isinstance(c, int) else pl.multiple_of(c * CW, CW), CW)
+        grad = lax.dot_general(gpre[...], wg[cols, :], NT, preferred_element_type=F32)
+        grad = grad + lax.dot_general(upre[...], wu[cols, :], NT, preferred_element_type=F32)
+        bsend[:, pl.ds(c * blk if isinstance(c, int) else pl.multiple_of(c * blk, blk), blk), :] = pack(grad, ne, cap)
+        total = jnp.sum(grad * xa[1, :, cols].astype(F32), axis=0, keepdims=True)
+        gsend[pl.ds(c, 1), :] = total / gain_in[:, cols]
+
+    def backward_send(c):
+        give_back(bsend, brecv, c, b_ss, b_rs.at[c])
+
+    held = chunks * 9 // 14
+
+    backward_chunk(0)
+    backward_send(0)
     dots = jnp.sum(g * act_a[...], axis=1, keepdims=True)
     dots = jnp.broadcast_to(dots, (rows, 128)).reshape(ne, cap, 128)
     place = lax.broadcasted_iota(jnp.int32, (ne, cap, 128), 1)
@@ -280,59 +327,32 @@
             device_id=(s, t, d), device_id_type=MESH,
         ).start()
     pltpu.make_async_copy(isend.at[e], irecv.at[e], i_rs).start()
-    gsend[...] = jnp.zeros_like(gsend)
-
-    def backward_chunk(c):
-        cols = pl.ds(pl.multiple_of(c * CW, CW), CW)
-        grad = lax.dot_general(gpre[...], wg[cols, :], NT, preferred_element_type=F32)
-        grad = grad + lax.dot_general(upre[...], wu[cols, :], NT, preferred_element_type=F32)
-        bsend[:, pl.ds(pl.multiple_of(c * blk, blk), blk), :] = pack(grad, ne, cap)
-        total = jnp.sum(grad * xa[1, :, cols].astype(F32), axis=0, keepdims=True)
-        gsend[pl.ds(c, 1), :] = total / gain_in[:, cols]
-
-    def backward_send(c):
-        give_back(bsend, brecv, c, b_ss, b_rs.at[c])
-
-    held = chunks * 9 // 14
-
-    @pl.loop(0, held)
+    forward_chunk(chunks - 1)
+
+    @pl.loop(1, held)
     def _(c):
         backward_chunk(c)
         backward_send(c)
 
-        @pl.when(c == 1)
-        def _():
-            forward_chunk(chunks - 1)
-
     pl.loop(held, chunks)(backward_chunk)
-    for t in plane:
-        pltpu.make_async_remote_copy(
-            src_ref=gsend, dst_ref=grecv.at[e], send_sem=g_ss.at[0], recv_sem=g_rs.at[0],
-            device_id=(s, t, d), device_id_type=MESH,
-        ).start()
-    pltpu.make_async_copy(gsend, grecv.at[e], g_rs.at[0]).start()
+    def share(stage, src, index, others):
+        for t in others:
+            pltpu.make_async_remote_copy(
+                src_ref=src, dst_ref=grecv.at[stage, index],
+                send_sem=g_ss.at[stage], recv_sem=g_rs.at[stage],
+                device_id=(s, t, d), device_id_type=MESH,
+            ).start()
+        pltpu.make_async_copy(src, grecv.at[stage, index], g_rs.at[stage]).start()
+
+    def shared(stage):
+        pltpu.make_async_copy(grecv.at[stage], grecv.at[stage], g_rs.at[stage]).wait()
+        return jnp.sum(grecv[stage], axis=0)
+
+    share(0, gsend, y, [lax.rem(y + k, ny) * nx + x for k in range(1, ny)])
     pl.loop(held, chunks)(backward_send)
 
-    def picked(recv, c, gather):
-        cube = recv[:, pl.ds(pl.multiple_of(c * blk, blk), blk), :].astype(F32)
-        cube = cube.reshape(experts, 2, blk, HW)
-        both = (cube[:, 0] + cube[:, 1]).astype(BF16).astype(F32)
-        rows_in = unpack(both, experts, cap).astype(BF16)
-        return jnp.dot(gather[:, :slots], rows_in, preferred_element_type=F32)
-
-    pltpu.make_async_copy(frecv, frecv, f_rs).wait()
-
-    @pl.loop(0, chunks)
-    def _(c):
-        cols = pl.ds(pl.multiple_of(c * CW, CW), CW)
-        mixed = wcol_f[:, :1] * picked(frecv, c, f_st)
-        lout[:, cols] = (fx[:, cols].astype(F32) + mixed).astype(BF16)
-
-    f_shift = pltpu.make_async_remote_copy(
-        src_ref=lout, dst_ref=fnext, send_sem=sh_ss, recv_sem=sh_rs,
-        device_id=after, device_id_type=MESH,
-    )
-    f_shift.start()
+    pl.loop(chunks - LAG, chunks)(forward_take)
+    f_shifts[1].start()
 
     pltpu.make_async_copy(irecv, irecv, i_rs).wait()
     per_expert = jnp.sum(irecv[...].reshape(experts, 2, 8, 128), axis=1)
@@ -361,19 +381,21 @@
         tgrad[:, cols] = (ct[:, cols].astype(F32) + grad).astype(BF16)
         shift_chunk(c).start()
 
-    pl.loop(0, held)(take)
-
-    pltpu.make_async_copy(grecv, grecv, g_rs.at[0]).wait()
-    gsend2[...] = jnp.sum(grecv[...], axis=0)
+    pl.loop(0, held // 2 + 1)(take)
+
+    gsend2[...] = shared(0)
+    share(1, gsend2, x, [y * nx + lax.rem(x + k, nx) for k in range(1, nx)])
+    pl.loop(held // 2 + 1, held + 1)(take)
+    gsend3[...] = shared(1)
     across = pltpu.make_async_remote_copy(
-        src_ref=gsend2, dst_ref=grecv2, send_sem=g_ss.at[1], recv_sem=g_rs.at[1],
+        src_ref=gsend3, dst_ref=grecv2, send_sem=g_ss.at[2], recv_sem=g_rs.at[2],
         device_id=replica, device_id_type=MESH,
     )
     across.start()
-    pl.loop(held, chunks)(take)
+    pl.loop(held + 1, chunks)(take)
     across.wait()
     for c in range(chunks):
-        gain_out[:, c * CW : (c + 1) * CW] = gsend2[c : c + 1, :] + grecv2[c : c + 1, :]
+        gain_out[:, c * CW : (c + 1) * CW] = gsend3[c : c + 1, :] + grecv2[c : c + 1, :]
 
     for j in range(3 * chunks):
         weight_copy(j).wait_send()
@@ -384,9 +406,12 @@
         ).wait()
     for buf, sem in ((fsend, f_ss), (bsend, b_ss)):
         pltpu.make_async_copy(buf.at[pl.ds(0, others)], buf.at[pl.ds(0, others)], sem).wait()
-    pltpu.make_async_copy(grecv.at[pl.ds(0, others)], grecv.at[pl.ds(0, others)], g_ss.at[0]).wait()
+    for stage, count in ((0, ny - 1), (1, nx - 1)):
+        sent = grecv.at[stage, pl.ds(0, count)]
+        pltpu.make_async_copy(sent, sent, g_ss.at[stage]).wait()
     pltpu.make_async_copy(isend.at[pl.ds(0, others)], isend.at[pl.ds(0, others)], i_ss).wait()
-    f_shift.wait()
+    for shift in f_shifts:
+        shift.wait()
     for c in range(chunks):
         shift_chunk(c).wait()
 
@@ -439,7 +464,8 @@
         pltpu.VMEM((ne, 8, 128), F32),
         pltpu.VMEM((16, CW), F32),
         pltpu.VMEM((16, CW), F32),
-        pltpu.VMEM((ne, 16, CW), F32),
+        pltpu.VMEM((16, CW), F32),
+        pltpu.VMEM((2, max(ny, nx), 16, CW), F32),
         pltpu.VMEM((16, CW), F32),
         sem((6,)),
         sem((3 * chunks,)),
@@ -447,17 +473,17 @@
         sem((3,)),
         sem((3,)),
         sem,
-        sem,
+        sem((chunks,)),
         sem,
         sem((chunks,)),
-        sem,
-        sem,
+        sem((2,)),
+        sem((2,)),
         sem((chunks,)),
         sem((chunks,)),
         sem,
         sem,
-        sem((2,)),
-        sem((2,)),
+        sem((3,)),
+        sem((3,)),
     ]
     fnext, bnext, gain = pl.pallas_call(
         functools.partial(body, sizes),

time: 297 us -> 298 us (level)
  no operation moved by 1% of the time
where the time goes in v4:
time: 298 us; the launch traced here: 296 us
  Pallas kernels  292 us (98%)
  local copies, waits for them, and re-layouts  3.77 us (1%)
    pallas_call x1, Pallas kernels, on_device(): pl.pallas_call(functools.partial(body, sizes), out_shape=[jax.ShapeDtypeS...  292 us

profile of v4, /device:TPU:2, one launch (start us, length us, event | category | flops | bytes accessed | tf_op | source)
XLA Modules:
  0.0 296.2 jit_solution(13170377282230788504)
XLA Ops:
  0.6 291.8 %shard_map.130 = (bf16[128,3584]{1,0:T(8,128)(2,1)}, bf16[128,3584]{1,0:T(8,128)(2,1)}, f32[1,3584]{1,0:T(1,128)}) custom-call(bf16[128,3584]{1,0:T(8,128)(2,1)} %bitcast.17, bf16[128,3584]{1,0:T(8,128)(2,1)} %bitcast.18, bf16[128,3584]{1,0:T(8,128)(2,1)} %bitcast.19, s32[1,128]{1,0:T(1,128)} %bitcast.20, s32[1,128]{1,0:T(1,128)} %bitcast.21, ...), custom_call_target="tpu_custom_call" | custom-call | tf_op jit(solution)/shard_map/pallas_call | solution.py:488
  292.5 0.0 copy-start
  292.5 0.0 copy-start.1
  292.5 2.2 copy.17
  294.7 0.0 copy-done
  294.7 0.9 copy.18
  295.6 0.0 copy-done.1
  295.6 0.6 copy.19
Async XLA Ops:
  292.5 2.3 copy-start
  292.5 3.2 %copy-start.1 = (f32[1,3584]{1,0:T(1,128)S(1)}, f32[1,3584]{1,0:T(1,128)}, u32[]{:S(2)}) copy-start(f32[1,3584]{1,0:T(1,128)} %get-tuple-element.14) | copy-start | bytes 43012
